TPU v7x, 1024 devices: a whole 4x8x16 slice. The times are simulated.
1024 devices in a mesh: blk: 128 (over z_lo, x, y), grp: 8 (over z_hi, core).
Axes of the slice: x: 4, y: 8, z: 16 (z_hi: 4, z_lo: 4; z = z_hi * 4 + z_lo), core: 2. Of those that a mesh axis runs over, the one named last changes fastest.
Arguments:
- image_emb: float32 [262144, 768], P(('blk', 'grp')), may hold values from -0.25 to 0.25
- text_emb: float32 [262144, 768], P(('blk', 'grp')), may hold values from -0.25 to 0.25
- labels: int32 [262144], P(('blk', 'grp')), may hold values from 0 to 255
- logit_scale: float32 [1], replicated, may hold values from 40 to 80
- logit_bias: float32 [1], replicated, may hold values from -9 to -4
Outputs:
- image_grad: float32 [262144, 768], P(('blk', 'grp'))
- text_grad: float32 [262144, 768], P(('blk', 'grp'))
All inputs are finite; a program needn't handle non-finite values.
Results may differ from a plain program's by a relative error of at most 0.0003.
Values sent between devices are 32-bit elements; how exact they have to be, the bound alone decides.
No kernel may reach another device: no remote copies, remote signals or barrier semaphores. Data moves between devices by JAX's collectives and lax.ppermute only.
A program may use at most 32 MiB of HBM per device.

v0:
```python
import jax
import jax.numpy as jnp
from jax import lax
from jax.sharding import PartitionSpec as P

EPS = 1e-06
HIGH = lax.Precision.HIGHEST


def swapped(value, axis, distance):
    mask = 2**distance
    pairs = [(source, source ^ mask) for source in range(lax.axis_size(axis))]
    return lax.ppermute(value, axis, pairs)


def unit_rows(rows):
    return rows * lax.rsqrt(jnp.sum(rows * rows, -1, keepdims=True) + EPS)


def norm_backward(rows, grad):
    inverse = lax.rsqrt(jnp.sum(rows * rows, -1, keepdims=True) + EPS)
    unit = rows * inverse
    return inverse * (grad - unit * jnp.sum(unit * grad, -1, keepdims=True))


def forward_grp(held):
    return swapped(held, "grp", lax.axis_size("grp").bit_length() - 2)


def forward_blk(held):
    return swapped(held, "blk", lax.axis_size("blk").bit_length() - 2)


def return_grp(part):
    return swapped(part, "grp", lax.axis_size("grp").bit_length() - 2)


def return_blk(part):
    return swapped(part, "blk", lax.axis_size("blk").bit_length() - 2)


def shards(image_emb, text_emb, labels, logit_scale, logit_bias):
    scale = logit_scale[0]
    bias = logit_bias[0]
    rows = image_emb.shape[0]
    image_unit = unit_rows(image_emb)
    text_unit = unit_rows(text_emb)
    columns = jnp.arange(rows, dtype=jnp.int32)
    own_slot = (jnp.arange(4, dtype=jnp.int32) == 0).astype(jnp.float32)[:, None, None]
    positive = (labels[:, None] == columns[None, :]).astype(jnp.float32)[None] * own_slot
    sections = (forward_grp, forward_blk)
    backs = (return_grp, return_blk)
    held = text_unit[None]
    for section in sections:
        held = jnp.concatenate([held, section(held)], 0)
    logits = scale * jnp.einsum("rd,mcd->mrc", image_unit, held, precision=HIGH) + bias
    slope = jax.nn.sigmoid(logits) - positive
    grad_image = scale * jnp.einsum("mrc,mcd->rd", slope, held, precision=HIGH)
    partial_text = scale * jnp.einsum("mrc,rd->mcd", slope, image_unit, precision=HIGH)
    folded = partial_text[0:2] + backs[1](partial_text[2:4])
    grad_text = folded[0] + backs[0](folded[1])
    return (norm_backward(image_emb, grad_image), norm_backward(text_emb, grad_text))


def solution(mesh):
    in_specs = (P(("blk", "grp"), None), P(("blk", "grp"), None), P(("blk", "grp")), P(), P())
    out_specs = (P(("blk", "grp"), None), P(("blk", "grp"), None))
    return jax.shard_map(shards, mesh=mesh, in_specs=in_specs, out_specs=out_specs, check_vma=False)
```

profile of v0, /device:TPU:1, one launch (start us, length us, event | category | flops | bytes accessed | tf_op | source)
XLA Modules:
  0.0 319.6 jit_solution(17662470624907771246)
XLA Ops:
  0.6 1.3 multiply_reduce_fusion.2
  1.9 1.3 multiply_bitcast_fusion
  3.2 0.0 copy-start.1
  3.2 0.0 copy-start.2
  3.2 20.0 %collective-permute-start = (f32[1,256,768]{2,1,0:T(8,128)S(1)}, f32[1,256,768]{2,1,0:T(8,128)S(1)}, u32[]{:S(2)}, u32[]{:S(2)}) collective-permute-start(f32[1,256,768]{2,1,0:T(8,128)S(1)} %multiply_bitcast_fusion), channel_id=1, source_target_pairs={{0,4},{1,5},{2,6},{3,7},{4,0},{5,1},{6,2},{7,3},{8,12},{9,13},{10,... | collective-permute-start | bytes 2359304 | tf_op jit(solution)/shard_map/ppermute | solution.py:13
  23.2 17.7 %collective-permute-done = f32[1,256,768]{2,1,0:T(8,128)S(1)} collective-permute-done((f32[1,256,768]{2,1,0:T(8,128)S(1)}, f32[1,256,768]{2,1,0:T(8,128)S(1)}, u32[]{:S(2)}, u32[]{:S(2)}) %collective-permute-start) | collective-permute-done | bytes 786464 | tf_op jit(solution)/shard_map/ppermute | solution.py:13
  41.0 0.1 pad_maximum_fusion.3
  41.1 25.1 %collective-permute-start.1 = (f32[2,256,768]{2,1,0:T(8,128)S(1)}, f32[2,256,768]{2,1,0:T(8,128)S(1)}, u32[]{:S(2)}, u32[]{:S(2)}) collective-permute-start(f32[2,256,768]{2,1,0:T(8,128)S(1)} %pad_maximum_fusion.3), channel_id=1, source_target_pairs={{0,512},{8,520},{16,528},{24,536},{32,544},{40,552},{48,560},{56,5... | collective-permute-start | bytes 4718600 | tf_op jit(solution)/shard_map/ppermute | solution.py:13
  67.5 0.1 multiply_reduce_fusion.3
  67.7 92.9 %collective-permute-done.1 = f32[2,256,768]{2,1,0:T(8,128)S(1)} collective-permute-done((f32[2,256,768]{2,1,0:T(8,128)S(1)}, f32[2,256,768]{2,1,0:T(8,128)S(1)}, u32[]{:S(2)}, u32[]{:S(2)}) %collective-permute-start.1) | collective-permute-done | bytes 1572896 | tf_op jit(solution)/shard_map/ppermute | solution.py:13
  160.6 2.9 fusion.11
  163.5 3.1 convolution_multiply_fusion
  166.6 0.1 slice.17
  166.7 1.9 collective-permute-start.2
  168.6 69.0 %collective-permute-done.2 = f32[2,256,768]{2,1,0:T(8,128)S(1)} collective-permute-done((f32[2,256,768]{2,1,0:T(8,128)S(1)}, f32[2,256,768]{2,1,0:T(8,128)S(1)}, u32[]{:S(2)}, u32[]{:S(2)}) %collective-permute-start.2) | collective-permute-done | bytes 1572896 | tf_op jit(solution)/shard_map/ppermute | solution.py:13
  237.7 0.2 slice_add_fusion
  237.9 0.1 slice_bitcast_fusion
  237.9 5.4 %collective-permute-start.3 = (f32[256,768]{1,0:T(8,128)S(1)}, f32[256,768]{1,0:T(8,128)S(1)}, u32[]{:S(2)}, u32[]{:S(2)}) collective-permute-start(f32[256,768]{1,0:T(8,128)S(1)} %slice_bitcast_fusion), channel_id=1, source_target_pairs={{0,4},{1,5},{2,6},{3,7},{4,0},{5,1},{6,2},{7,3},{8,12},{9,13},{10,... | collective-permute-start | bytes 2359304 | tf_op jit(solution)/shard_map/ppermute | solution.py:13
  243.4 3.2 %multiply_reduce_fusion.1 = (f32[256]{0:T(256)S(1)}, f32[256,768]{1,0:T(8,128)S(1)}) fusion(f32[256,768]{1,0:T(8,128)S(1)} %copy-done.1, f32[256]{0:T(256)S(1)} %add_rsqrt_fusion.1, f32[4,256,256]{1,2,0:T(8,128)S(1)} %fusion.11, f32[2,256,768]{2,1,0:T(8,128)S(1)} %collective-permute-done.1, f32[1,256,768]{2,1,0:T(8,128)S(1)} %collective-permute-done, ...), kind=kOutput, calls=%fused_computation.24 | convolution fusion | flops 2418278144 | bytes 5769220 | tf_op jit(solution)/shard_map/mrc,mcd->rd/dot_general | solution.py:58
  246.6 0.0 copy-start
  246.6 1.1 subtract_multiply_fusion.1
  247.7 70.5 %collective-permute-done.3 = f32[256,768]{1,0:T(8,128)S(1)} collective-permute-done((f32[256,768]{1,0:T(8,128)S(1)}, f32[256,768]{1,0:T(8,128)S(1)}, u32[]{:S(2)}, u32[]{:S(2)}) %collective-permute-start.3) | collective-permute-done | bytes 786464 | tf_op jit(solution)/shard_map/ppermute | solution.py:13
  318.2 0.3 multiply_reduce_fusion
  318.5 1.1 subtract_multiply_fusion
  (7 shorter events, 0.1 us)
Async XLA Ops:
  3.2 64.3 %copy-start.1 = (f32[256,768]{1,0:T(8,128)S(1)}, f32[256,768]{1,0:T(8,128)}, u32[]{:S(2)}) copy-start(f32[256,768]{1,0:T(8,128)} %param.5) | copy-start | bytes 2359300
  3.2 64.5 %copy-start.2 = (s32[256]{0:T(256)S(1)}, s32[256]{0:T(256)}, u32[]{:S(2)}) copy-start(s32[256]{0:T(256)} %param.7) | copy-start | bytes 3076
  3.2 37.8 %collective-permute-start = (f32[1,256,768]{2,1,0:T(8,128)S(1)}, f32[1,256,768]{2,1,0:T(8,128)S(1)}, u32[]{:S(2)}, u32[]{:S(2)}) collective-permute-start(f32[1,256,768]{2,1,0:T(8,128)S(1)} %multiply_bitcast_fusion), channel_id=1, source_target_pairs={{0,4},{1,5},{2,6},{3,7},{4,0},{5,1},{6,2},{7,3},{8,12},{9,13},{10,... | collective-permute-start | bytes 2359304 | tf_op jit(solution)/shard_map/ppermute | solution.py:13
  41.1 119.5 %collective-permute-start.1 = (f32[2,256,768]{2,1,0:T(8,128)S(1)}, f32[2,256,768]{2,1,0:T(8,128)S(1)}, u32[]{:S(2)}, u32[]{:S(2)}) collective-permute-start(f32[2,256,768]{2,1,0:T(8,128)S(1)} %pad_maximum_fusion.3), channel_id=1, source_target_pairs={{0,512},{8,520},{16,528},{24,536},{32,544},{40,552},{48,560},{56,5... | collective-permute-start | bytes 4718600 | tf_op jit(solution)/shard_map/ppermute | solution.py:13
  166.7 71.0 %collective-permute-start.2 = (f32[2,256,768]{2,1,0:T(8,128)S(1)}, f32[2,256,768]{2,1,0:T(8,128)S(1)}, u32[]{:S(2)}, u32[]{:S(2)}) collective-permute-start(f32[2,256,768]{2,1,0:T(8,128)S(1)} %slice.17), channel_id=1, source_target_pairs={{0,512},{8,520},{16,528},{24,536},{32,544},{40,552},{48,560},{56,5... | collective-permute-start | bytes 4718600 | tf_op jit(solution)/shard_map/ppermute | solution.py:13
  237.9 80.2 %collective-permute-start.3 = (f32[256,768]{1,0:T(8,128)S(1)}, f32[256,768]{1,0:T(8,128)S(1)}, u32[]{:S(2)}, u32[]{:S(2)}) collective-permute-start(f32[256,768]{1,0:T(8,128)S(1)} %slice_bitcast_fusion), channel_id=1, source_target_pairs={{0,4},{1,5},{2,6},{3,7},{4,0},{5,1},{6,2},{7,3},{8,12},{9,13},{10,... | collective-permute-start | bytes 2359304 | tf_op jit(solution)/shard_map/ppermute | solution.py:13
  246.6 71.6 %copy-start = (f32[256,768]{1,0:T(8,128)S(1)}, f32[256,768]{1,0:T(8,128)}, u32[]{:S(2)}) copy-start(f32[256,768]{1,0:T(8,128)} %param.6) | copy-start | bytes 2359300
where the time goes:
time: 320 us
  waiting for transfers between devices  250 us (78%)
  starting transfers between devices  52.5 us (16%)
  matrix products  9.18 us (3%)
  other arithmetic  5.44 us (2%)
    ppermute x4, waiting for transfers between devices, swapped(): return lax.ppermute(value, axis, pairs)  250 us
    ppermute x4, starting transfers between devices, swapped(): return lax.ppermute(value, axis, pairs)  52.5 us
  transfers between devices with their start and end apart: 4, of which 4 were waited for; matrix products, arithmetic and copies ran while one was open for 1% of the time, Pallas kernels for 0%

commit v1 on v0

v1 whole, which is shorter than its diff:
```python
import jax
import jax.numpy as jnp
from jax import lax
from jax.sharding import PartitionSpec as P

EPS = 1e-06
HIGH = lax.Precision.HIGHEST
AXES = ("blk", "grp")
CHUNKS = 4


def exchanged(value, flip):
    size = lax.axis_size("blk") * lax.axis_size("grp")
    return lax.ppermute(value, AXES, [(source, source ^ flip) for source in range(size)])


def unit_rows(rows):
    return rows * lax.rsqrt(jnp.sum(rows * rows, -1, keepdims=True) + EPS)


def norm_backward(rows, grad):
    inverse = lax.rsqrt(jnp.sum(rows * rows, -1, keepdims=True) + EPS)
    unit = rows * inverse
    return inverse * (grad - unit * jnp.sum(unit * grad, -1, keepdims=True))


def shards(image_emb, text_emb, labels, logit_scale, logit_bias):
    scale = logit_scale[0]
    bias = logit_bias[0]
    rows = image_emb.shape[0]
    n_grp = lax.axis_size("grp")
    near = (lax.axis_size("blk") // 2) * n_grp
    far = near + n_grp // 2
    part = rows // CHUNKS

    far_images = [exchanged(image_emb[i * part:(i + 1) * part], far) for i in range(CHUNKS)]
    near_text = exchanged(text_emb, near)

    texts = jnp.concatenate([unit_rows(text_emb), unit_rows(near_text)], 0)
    columns = jnp.arange(2 * rows, dtype=jnp.int32)

    def tile(images, marks):
        logits = scale * jnp.einsum("rd,cd->rc", images, texts, precision=HIGH) + bias
        slope = jax.nn.sigmoid(logits)
        if marks is not None:
            slope = slope - (marks[:, None] == columns[None, :]).astype(jnp.float32)
        grad_image = scale * jnp.einsum("rc,cd->rd", slope, texts, precision=HIGH)
        grad_text = scale * jnp.einsum("rc,rd->cd", slope, images, precision=HIGH)
        return grad_image, grad_text

    own_image_grad, text_grads = tile(unit_rows(image_emb), labels)
    returned = []
    for chunk in far_images:
        grad_image, grad_text = tile(unit_rows(chunk), None)
        returned.append(exchanged(grad_image, far))
        text_grads = text_grads + grad_text
    near_back = exchanged(text_grads[rows:], near)
    grad_image = own_image_grad + jnp.concatenate(returned, 0)
    grad_text = text_grads[:rows] + near_back
    return (norm_backward(image_emb, grad_image), norm_backward(text_emb, grad_text))


def solution(mesh):
    in_specs = (P(("blk", "grp"), None), P(("blk", "grp"), None), P(("blk", "grp")), P(), P())
    out_specs = (P(("blk", "grp"), None), P(("blk", "grp"), None))
    return jax.shard_map(shards, mesh=mesh, in_specs=in_specs, out_specs=out_specs, check_vma=False)
```

time: 320 us -> 208 us (0.65)
  the two profiles are of different devices: /device:TPU:1 before, /device:TPU:64 now
where the time goes in v1:
time: 208 us
  waiting for transfers between devices  112 us (54%)
  starting transfers between devices  66.4 us (32%)
  matrix products  22.4 us (11%)
  other arithmetic  3.55 us (2%)
  between operations  2.22 us (1%)
    ppermute x10, waiting for transfers between devices, exchanged(): lax.ppermute(value, AXES, [(source, source ^ flip) for source in range(si...  112 us
    ppermute x10, starting transfers between devices, exchanged(): lax.ppermute(value, AXES, [(source, source ^ flip) for source in range(si...  66.4 us
    dot_general x5, matrix products, tile(): jnp.einsum('rd,cd->rc', images, texts, precision=HIGH)  8.43 us
    dot_general x5, matrix products, tile(): grad_text = scale * jnp.einsum('rc,rd->cd', slope, images, precision=HIGH)  8.05 us
    dot_general x5, matrix products, tile(): grad_image = scale * jnp.einsum('rc,cd->rd', slope, texts, precision=HIGH)  5.93 us
  transfers between devices with their start and end apart: 10, of which 9 were waited for; matrix products, arithmetic and copies ran while one was open for 2% of the time, Pallas kernels for 0%

profile of v1, /device:TPU:64, one launch (start us, length us, event | category | flops | bytes accessed | tf_op | source)
XLA Modules:
  0.0 207.8 jit_solution(14939088024615189261)
XLA Ops:
  2.0 18.5 %collective-permute-start.1 = (f32[64,768]{1,0:T(8,128)S(1)}, f32[64,768]{1,0:T(8,128)S(1)}, u32[]{:S(2)}, u32[]{:S(2)}) collective-permute-start(f32[64,768]{1,0:T(8,128)S(1)} %get-tuple-element.2), channel_id=1, source_target_pairs={{0,516},{1,517},{2,518},{3,519},{4,512},{5,513},{6,514},{7,515},{8... | collective-permute-start | bytes 589832 | tf_op jit(solution)/shard_map/ppermute | solution.py:14
  20.5 1.9 collective-permute-start.3
  22.5 10.8 %collective-permute-start.7 = (f32[64,768]{1,0:T(8,128)S(1)}, f32[64,768]{1,0:T(8,128)S(1)}, u32[]{:S(2)}, u32[]{:S(2)}) collective-permute-start(f32[64,768]{1,0:T(8,128)S(1)} %get-tuple-element.4), channel_id=1, source_target_pairs={{0,516},{1,517},{2,518},{3,519},{4,512},{5,513},{6,514},{7,515},{8... | collective-permute-start | bytes 589832 | tf_op jit(solution)/shard_map/ppermute | solution.py:14
  33.3 1.9 collective-permute-start.5
  35.2 2.5 %collective-permute-start = (f32[256,768]{1,0:T(8,128)S(1)}, f32[256,768]{1,0:T(8,128)S(1)}, u32[]{:S(2)}, u32[]{:S(2)}) collective-permute-start(f32[256,768]{1,0:T(8,128)S(1)} %copy-done.1), channel_id=1, source_target_pairs={{0,512},{1,513},{2,514},{3,515},{4,516},{5,517},{6,518},{7,519},{8... | collective-permute-start | bytes 2359304 | tf_op jit(solution)/shard_map/ppermute | solution.py:14
  39.4 4.0 %collective-permute-done.1 = f32[64,768]{1,0:T(8,128)S(1)} collective-permute-done((f32[64,768]{1,0:T(8,128)S(1)}, f32[64,768]{1,0:T(8,128)S(1)}, u32[]{:S(2)}, u32[]{:S(2)}) %collective-permute-start.1) | collective-permute-done | bytes 196640 | tf_op jit(solution)/shard_map/ppermute | solution.py:14
  43.5 10.8 %collective-permute-done.3 = f32[64,768]{1,0:T(8,128)S(1)} collective-permute-done((f32[64,768]{1,0:T(8,128)S(1)}, f32[64,768]{1,0:T(8,128)S(1)}, u32[]{:S(2)}, u32[]{:S(2)}) %collective-permute-start.3) | collective-permute-done | bytes 196640 | tf_op jit(solution)/shard_map/ppermute | solution.py:14
  54.5 4.3 %collective-permute-done.7 = f32[64,768]{1,0:T(8,128)S(1)} collective-permute-done((f32[64,768]{1,0:T(8,128)S(1)}, f32[64,768]{1,0:T(8,128)S(1)}, u32[]{:S(2)}, u32[]{:S(2)}) %collective-permute-start.7) | collective-permute-done | bytes 196640 | tf_op jit(solution)/shard_map/ppermute | solution.py:14
  58.9 6.4 %collective-permute-done.5 = f32[64,768]{1,0:T(8,128)S(1)} collective-permute-done((f32[64,768]{1,0:T(8,128)S(1)}, f32[64,768]{1,0:T(8,128)S(1)}, u32[]{:S(2)}, u32[]{:S(2)}) %collective-permute-start.5) | collective-permute-done | bytes 196640 | tf_op jit(solution)/shard_map/ppermute | solution.py:14
  65.4 34.8 %collective-permute-done = f32[256,768]{1,0:T(8,128)S(1)} collective-permute-done((f32[256,768]{1,0:T(8,128)S(1)}, f32[256,768]{1,0:T(8,128)S(1)}, u32[]{:S(2)}, u32[]{:S(2)}) %collective-permute-start) | collective-permute-done | bytes 786464 | tf_op jit(solution)/shard_map/ppermute | solution.py:14
  106.6 1.7 fusion.16
  109.4 1.7 fusion.21
  113.7 1.7 fusion.37
  115.4 1.7 fusion.26
  118.6 1.8 add_multiply_fusion
  120.4 5.3 %collective-permute-start.9 = (f32[256,768]{1,0:T(8,128)S(1)}, f32[256,768]{1,0:T(8,128)S(1)}, u32[]{:S(2)}, u32[]{:S(2)}) collective-permute-start(f32[256,768]{1,0:T(8,128)S(1)} %slice.25), channel_id=1, source_target_pairs={{0,512},{1,513},{2,514},{3,515},{4,516},{5,517},{6,518},{7,519},{8... | collective-permute-start | bytes 2359304 | tf_op jit(solution)/shard_map/ppermute | solution.py:14
  126.8 1.9 collective-permute-start.2
  128.7 10.8 %collective-permute-start.4 = (f32[64,768]{1,0:T(8,128)S(1)}, f32[64,768]{1,0:T(8,128)S(1)}, u32[]{:S(2)}, u32[]{:S(2)}) collective-permute-start(f32[64,768]{1,0:T(8,128)S(1)} %convolution_multiply_fusion.4), channel_id=1, source_target_pairs={{0,516},{1,517},{2,518},{3,519},{4,512},{5,513},{6,514},{7,515},{8... | collective-permute-start | bytes 589832 | tf_op jit(solution)/shard_map/ppermute | solution.py:14
  139.5 1.9 collective-permute-start.6
  141.5 10.8 %collective-permute-start.8 = (f32[64,768]{1,0:T(8,128)S(1)}, f32[64,768]{1,0:T(8,128)S(1)}, u32[]{:S(2)}, u32[]{:S(2)}) collective-permute-start(f32[64,768]{1,0:T(8,128)S(1)} %convolution_multiply_fusion.2), channel_id=1, source_target_pairs={{0,516},{1,517},{2,518},{3,519},{4,512},{5,513},{6,514},{7,515},{8... | collective-permute-start | bytes 589832 | tf_op jit(solution)/shard_map/ppermute | solution.py:14
  152.3 28.8 %collective-permute-done.2 = f32[64,768]{1,0:T(8,128)S(1)} collective-permute-done((f32[64,768]{1,0:T(8,128)S(1)}, f32[64,768]{1,0:T(8,128)S(1)}, u32[]{:S(2)}, u32[]{:S(2)}) %collective-permute-start.2) | collective-permute-done | bytes 196640 | tf_op jit(solution)/shard_map/ppermute | solution.py:14
  181.1 16.2 %collective-permute-done.4 = f32[64,768]{1,0:T(8,128)S(1)} collective-permute-done((f32[64,768]{1,0:T(8,128)S(1)}, f32[64,768]{1,0:T(8,128)S(1)}, u32[]{:S(2)}, u32[]{:S(2)}) %collective-permute-start.4) | collective-permute-done | bytes 196640 | tf_op jit(solution)/shard_map/ppermute | solution.py:14
  197.3 4.2 %collective-permute-done.6 = f32[64,768]{1,0:T(8,128)S(1)} collective-permute-done((f32[64,768]{1,0:T(8,128)S(1)}, f32[64,768]{1,0:T(8,128)S(1)}, u32[]{:S(2)}, u32[]{:S(2)}) %collective-permute-start.6) | collective-permute-done | bytes 196640 | tf_op jit(solution)/shard_map/ppermute | solution.py:14
  201.5 2.3 %collective-permute-done.8 = f32[64,768]{1,0:T(8,128)S(1)} collective-permute-done((f32[64,768]{1,0:T(8,128)S(1)}, f32[64,768]{1,0:T(8,128)S(1)}, u32[]{:S(2)}, u32[]{:S(2)}) %collective-permute-start.8) | collective-permute-done | bytes 196640 | tf_op jit(solution)/shard_map/ppermute | solution.py:14
  (38 shorter events, 18.9 us)
Async XLA Ops:
  0.6 37.2 %copy-start = (f32[256,768]{1,0:T(8,128)S(1)}, f32[256,768]{1,0:T(8,128)}, u32[]{:S(2)}) copy-start(f32[256,768]{1,0:T(8,128)} %param.5) | copy-start | bytes 2359300
  0.6 34.6 %copy-start.1 = (f32[256,768]{1,0:T(8,128)S(1)}, f32[256,768]{1,0:T(8,128)}, u32[]{:S(2)}) copy-start(f32[256,768]{1,0:T(8,128)} %param.6) | copy-start | bytes 2359300
  2.0 41.4 %collective-permute-start.1 = (f32[64,768]{1,0:T(8,128)S(1)}, f32[64,768]{1,0:T(8,128)S(1)}, u32[]{:S(2)}, u32[]{:S(2)}) collective-permute-start(f32[64,768]{1,0:T(8,128)S(1)} %get-tuple-element.2), channel_id=1, source_target_pairs={{0,516},{1,517},{2,518},{3,519},{4,512},{5,513},{6,514},{7,515},{8... | collective-permute-start | bytes 589832 | tf_op jit(solution)/shard_map/ppermute | solution.py:14
  20.5 33.8 %collective-permute-start.3 = (f32[64,768]{1,0:T(8,128)S(1)}, f32[64,768]{1,0:T(8,128)S(1)}, u32[]{:S(2)}, u32[]{:S(2)}) collective-permute-start(f32[64,768]{1,0:T(8,128)S(1)} %get-tuple-element.3), channel_id=1, source_target_pairs={{0,516},{1,517},{2,518},{3,519},{4,512},{5,513},{6,514},{7,515},{8... | collective-permute-start | bytes 589832 | tf_op jit(solution)/shard_map/ppermute | solution.py:14
  22.5 36.3 %collective-permute-start.7 = (f32[64,768]{1,0:T(8,128)S(1)}, f32[64,768]{1,0:T(8,128)S(1)}, u32[]{:S(2)}, u32[]{:S(2)}) collective-permute-start(f32[64,768]{1,0:T(8,128)S(1)} %get-tuple-element.4), channel_id=1, source_target_pairs={{0,516},{1,517},{2,518},{3,519},{4,512},{5,513},{6,514},{7,515},{8... | collective-permute-start | bytes 589832 | tf_op jit(solution)/shard_map/ppermute | solution.py:14
  33.3 32.0 %collective-permute-start.5 = (f32[64,768]{1,0:T(8,128)S(1)}, f32[64,768]{1,0:T(8,128)S(1)}, u32[]{:S(2)}, u32[]{:S(2)}) collective-permute-start(f32[64,768]{1,0:T(8,128)S(1)} %get-tuple-element.5), channel_id=1, source_target_pairs={{0,516},{1,517},{2,518},{3,519},{4,512},{5,513},{6,514},{7,515},{8... | collective-permute-start | bytes 589832 | tf_op jit(solution)/shard_map/ppermute | solution.py:14
  35.2 65.0 %collective-permute-start = (f32[256,768]{1,0:T(8,128)S(1)}, f32[256,768]{1,0:T(8,128)S(1)}, u32[]{:S(2)}, u32[]{:S(2)}) collective-permute-start(f32[256,768]{1,0:T(8,128)S(1)} %copy-done.1), channel_id=1, source_target_pairs={{0,512},{1,513},{2,514},{3,515},{4,516},{5,517},{6,518},{7,519},{8... | collective-permute-start | bytes 2359304 | tf_op jit(solution)/shard_map/ppermute | solution.py:14
  39.4 61.1 %copy-start.2 = (s32[256]{0:T(256)S(1)}, s32[256]{0:T(256)}, u32[]{:S(2)}) copy-start(s32[256]{0:T(256)} %param.7) | copy-start | bytes 3076
  120.4 86.1 %collective-permute-start.9 = (f32[256,768]{1,0:T(8,128)S(1)}, f32[256,768]{1,0:T(8,128)S(1)}, u32[]{:S(2)}, u32[]{:S(2)}) collective-permute-start(f32[256,768]{1,0:T(8,128)S(1)} %slice.25), channel_id=1, source_target_pairs={{0,512},{1,513},{2,514},{3,515},{4,516},{5,517},{6,518},{7,519},{8... | collective-permute-start | bytes 2359304 | tf_op jit(solution)/shard_map/ppermute | solution.py:14
  126.8 54.3 %collective-permute-start.2 = (f32[64,768]{1,0:T(8,128)S(1)}, f32[64,768]{1,0:T(8,128)S(1)}, u32[]{:S(2)}, u32[]{:S(2)}) collective-permute-start(f32[64,768]{1,0:T(8,128)S(1)} %convolution_multiply_fusion.5), channel_id=1, source_target_pairs={{0,516},{1,517},{2,518},{3,519},{4,512},{5,513},{6,514},{7,515},{8... | collective-permute-start | bytes 589832 | tf_op jit(solution)/shard_map/ppermute | solution.py:14
  128.7 68.6 %collective-permute-start.4 = (f32[64,768]{1,0:T(8,128)S(1)}, f32[64,768]{1,0:T(8,128)S(1)}, u32[]{:S(2)}, u32[]{:S(2)}) collective-permute-start(f32[64,768]{1,0:T(8,128)S(1)} %convolution_multiply_fusion.4), channel_id=1, source_target_pairs={{0,516},{1,517},{2,518},{3,519},{4,512},{5,513},{6,514},{7,515},{8... | collective-permute-start | bytes 589832 | tf_op jit(solution)/shard_map/ppermute | solution.py:14
  139.5 62.0 %collective-permute-start.6 = (f32[64,768]{1,0:T(8,128)S(1)}, f32[64,768]{1,0:T(8,128)S(1)}, u32[]{:S(2)}, u32[]{:S(2)}) collective-permute-start(f32[64,768]{1,0:T(8,128)S(1)} %convolution_multiply_fusion.3), channel_id=1, source_target_pairs={{0,516},{1,517},{2,518},{3,519},{4,512},{5,513},{6,514},{7,515},{8... | collective-permute-start | bytes 589832 | tf_op jit(solution)/shard_map/ppermute | solution.py:14
  141.5 62.3 %collective-permute-start.8 = (f32[64,768]{1,0:T(8,128)S(1)}, f32[64,768]{1,0:T(8,128)S(1)}, u32[]{:S(2)}, u32[]{:S(2)}) collective-permute-start(f32[64,768]{1,0:T(8,128)S(1)} %convolution_multiply_fusion.2), channel_id=1, source_target_pairs={{0,516},{1,517},{2,518},{3,519},{4,512},{5,513},{6,514},{7,515},{8... | collective-permute-start | bytes 589832 | tf_op jit(solution)/shard_map/ppermute | solution.py:14

commit v2 on v1

v2 whole, which is shorter than its diff:
```python
import jax
import jax.numpy as jnp
from jax import lax
from jax.sharding import PartitionSpec as P

EPS = 1e-06
HIGH = lax.Precision.HIGHEST
AXES = ("blk", "grp")


def exchanged(value, flip):
    size = lax.axis_size("blk") * lax.axis_size("grp")
    return lax.ppermute(value, AXES, [(source, source ^ flip) for source in range(size)])


def unit_rows(rows):
    return rows * lax.rsqrt(jnp.sum(rows * rows, -1, keepdims=True) + EPS)


def norm_backward(rows, grad):
    inverse = lax.rsqrt(jnp.sum(rows * rows, -1, keepdims=True) + EPS)
    unit = rows * inverse
    return inverse * (grad - unit * jnp.sum(unit * grad, -1, keepdims=True))


def times(a, b):
    return jnp.einsum("rc,cd->rd", a, b, precision=HIGH)


def times_transposed(a, b):
    return jnp.einsum("rc,rd->cd", a, b, precision=HIGH)


def shards(image_emb, text_emb, labels, logit_scale, logit_bias):
    scale = logit_scale[0]
    bias = logit_bias[0]
    rows = image_emb.shape[0]
    n_grp = lax.axis_size("grp")
    near = (lax.axis_size("blk") // 2) * n_grp
    far = near + n_grp // 2

    def slopes(images, texts):
        return jax.nn.sigmoid(scale * jnp.einsum("rd,cd->rc", images, texts, precision=HIGH) + bias)

    near_emb = exchanged(text_emb, near)
    far_emb = exchanged(image_emb, far)

    image, text = unit_rows(image_emb), unit_rows(text_emb)
    columns = jnp.arange(rows, dtype=jnp.int32)
    slope = slopes(image, text) - (labels[:, None] == columns[None, :]).astype(jnp.float32)
    image_grad = times(slope, text)
    text_grad = times_transposed(slope, image)

    near_text = unit_rows(near_emb)
    slope = slopes(image, near_text)
    image_grad = image_grad + times(slope, near_text)
    near_grad = times_transposed(slope, image)
    image_grad, text_grad, near_grad, near_text = lax.optimization_barrier((image_grad, text_grad, near_grad, near_text))

    far_image = unit_rows(far_emb)
    texts = jnp.concatenate([text, near_text], 0)
    slope = slopes(far_image, texts)
    far_grad, slope = lax.optimization_barrier((scale * times(slope, texts), slope))
    far_back = exchanged(far_grad, far)
    near_back = exchanged(scale * (near_grad + times_transposed(slope[:, rows:], far_image)), near)
    text_grad = scale * (text_grad + times_transposed(slope[:, :rows], far_image))
    return (norm_backward(image_emb, scale * image_grad + far_back), norm_backward(text_emb, text_grad + near_back))


def solution(mesh):
    in_specs = (P(("blk", "grp"), None), P(("blk", "grp"), None), P(("blk", "grp")), P(), P())
    out_specs = (P(("blk", "grp"), None), P(("blk", "grp"), None))
    return jax.shard_map(shards, mesh=mesh, in_specs=in_specs, out_specs=out_specs, check_vma=False)
```

time: 208 us -> 166 us (0.80)
  the two profiles are of different devices: /device:TPU:64 before, /device:TPU:253 now
where the time goes in v2:
time: 166 us
  waiting for transfers between devices  116 us (70%)
  starting transfers between devices  31.8 us (19%)
  matrix products  10.5 us (6%)
  other arithmetic  4.72 us (3%)
  between operations  2.13 us (1%)
    ppermute x4, waiting for transfers between devices, exchanged(): lax.ppermute(value, AXES, [(source, source ^ flip) for source in range(si...  116 us
    ppermute x4, starting transfers between devices, exchanged(): lax.ppermute(value, AXES, [(source, source ^ flip) for source in range(si...  31.8 us
    dot_general x4, matrix products, times_transposed(): return jnp.einsum('rc,rd->cd', a, b, precision=HIGH)  3.88 us
    dot_general x3, matrix products, slopes(): jnp.einsum('rd,cd->rc', images, texts, precision=HIGH)  3.42 us
  transfers between devices with their start and end apart: 4, of which 4 were waited for; matrix products, arithmetic and copies ran while one was open for 6% of the time, Pallas kernels for 0%

profile of v2, /device:TPU:253, one launch (start us, length us, event | category | flops | bytes accessed | tf_op | source)
XLA Modules:
  0.0 166.0 jit_solution(11076503620939041342)
XLA Ops:
  0.6 2.1 %collective-permute-start = (f32[256,768]{1,0:T(8,128)}, f32[256,768]{1,0:T(8,128)S(1)}, u32[]{:S(2)}, u32[]{:S(2)}) collective-permute-start(f32[256,768]{1,0:T(8,128)} %param.6), channel_id=1, source_target_pairs={{0,512},{1,513},{2,514},{3,515},{4,516},{5,517},{6,518},{7,519},{8... | collective-permute-start | bytes 2359304 | tf_op jit(solution)/shard_map/ppermute | solution.py:13
  2.7 16.7 %collective-permute-start.1 = (f32[256,768]{1,0:T(8,128)}, f32[256,768]{1,0:T(8,128)S(1)}, u32[]{:S(2)}, u32[]{:S(2)}) collective-permute-start(f32[256,768]{1,0:T(8,128)} %param.5), channel_id=1, source_target_pairs={{0,516},{1,517},{2,518},{3,519},{4,512},{5,513},{6,514},{7,515},{8... | collective-permute-start | bytes 2359304 | tf_op jit(solution)/shard_map/ppermute | solution.py:13
  19.4 1.3 multiply_reduce_fusion.4
  22.2 0.5 copy-done.2
  22.8 0.9 fusion.13
  23.7 0.8 fusion.40
  24.5 1.0 fusion.25
  25.5 18.0 %collective-permute-done = f32[256,768]{1,0:T(8,128)S(1)} collective-permute-done((f32[256,768]{1,0:T(8,128)}, f32[256,768]{1,0:T(8,128)S(1)}, u32[]{:S(2)}, u32[]{:S(2)}) %collective-permute-start) | collective-permute-done | bytes 786464 | tf_op jit(solution)/shard_map/ppermute | solution.py:13
  43.7 0.9 fusion.17
  44.6 1.0 fusion.23
  45.6 0.8 convolution_add_fusion
  46.4 56.6 %collective-permute-done.1 = f32[256,768]{1,0:T(8,128)S(1)} collective-permute-done((f32[256,768]{1,0:T(8,128)}, f32[256,768]{1,0:T(8,128)S(1)}, u32[]{:S(2)}, u32[]{:S(2)}) %collective-permute-start.1) | collective-permute-done | bytes 786464 | tf_op jit(solution)/shard_map/ppermute | solution.py:13
  103.2 1.7 fusion.6
  104.8 1.5 convolution_multiply_fusion
  106.3 1.0 fusion.18
  107.4 1.9 %collective-permute-start.3 = (f32[256,768]{1,0:T(8,128)S(1)}, f32[256,768]{1,0:T(8,128)S(1)}, u32[]{:S(2)}, u32[]{:S(2)}) collective-permute-start(f32[256,768]{1,0:T(8,128)S(1)} %add_multiply_fusion), channel_id=1, source_target_pairs={{0,512},{1,513},{2,514},{3,515},{4,516},{5,517},{6,518},{7,519},{8... | collective-permute-start | bytes 2359304 | tf_op jit(solution)/shard_map/ppermute | solution.py:13
  109.4 11.2 %collective-permute-start.2 = (f32[256,768]{1,0:T(8,128)S(1)}, f32[256,768]{1,0:T(8,128)S(1)}, u32[]{:S(2)}, u32[]{:S(2)}) collective-permute-start(f32[256,768]{1,0:T(8,128)S(1)} %convolution_multiply_fusion), channel_id=1, source_target_pairs={{0,516},{1,517},{2,518},{3,519},{4,512},{5,513},{6,514},{7,515},{8... | collective-permute-start | bytes 2359304 | tf_op jit(solution)/shard_map/ppermute | solution.py:13
  120.6 1.0 fusion.20
  121.6 32.3 %collective-permute-done.3 = f32[256,768]{1,0:T(8,128)S(1)} collective-permute-done((f32[256,768]{1,0:T(8,128)S(1)}, f32[256,768]{1,0:T(8,128)S(1)}, u32[]{:S(2)}, u32[]{:S(2)}) %collective-permute-start.3) | collective-permute-done | bytes 786464 | tf_op jit(solution)/shard_map/ppermute | solution.py:13
  153.9 0.3 multiply_reduce_fusion
  154.1 1.1 subtract_multiply_fusion
  155.2 9.5 %collective-permute-done.2 = f32[256,768]{1,0:T(8,128)S(1)} collective-permute-done((f32[256,768]{1,0:T(8,128)S(1)}, f32[256,768]{1,0:T(8,128)S(1)}, u32[]{:S(2)}, u32[]{:S(2)}) %collective-permute-start.2) | collective-permute-done | bytes 786464 | tf_op jit(solution)/shard_map/ppermute | solution.py:13
  164.7 0.3 multiply_reduce_fusion.1
  164.9 1.1 subtract_multiply_fusion.1
  (15 shorter events, 0.8 us)
Async XLA Ops:
  0.6 20.0 %copy-start = (f32[256,768]{1,0:T(8,128)S(1)}, f32[256,768]{1,0:T(8,128)}, u32[]{:S(2)}) copy-start(f32[256,768]{1,0:T(8,128)} %param.5) | copy-start | bytes 2359300
  0.6 21.5 %copy-start.1 = (f32[256,768]{1,0:T(8,128)S(1)}, f32[256,768]{1,0:T(8,128)}, u32[]{:S(2)}) copy-start(f32[256,768]{1,0:T(8,128)} %param.6) | copy-start | bytes 2359300
  0.6 42.8 %collective-permute-start = (f32[256,768]{1,0:T(8,128)}, f32[256,768]{1,0:T(8,128)S(1)}, u32[]{:S(2)}, u32[]{:S(2)}) collective-permute-start(f32[256,768]{1,0:T(8,128)} %param.6), channel_id=1, source_target_pairs={{0,512},{1,513},{2,514},{3,515},{4,516},{5,517},{6,518},{7,519},{8... | collective-permute-start | bytes 2359304 | tf_op jit(solution)/shard_map/ppermute | solution.py:13
  2.7 100.3 %collective-permute-start.1 = (f32[256,768]{1,0:T(8,128)}, f32[256,768]{1,0:T(8,128)S(1)}, u32[]{:S(2)}, u32[]{:S(2)}) collective-permute-start(f32[256,768]{1,0:T(8,128)} %param.5), channel_id=1, source_target_pairs={{0,516},{1,517},{2,518},{3,519},{4,512},{5,513},{6,514},{7,515},{8... | collective-permute-start | bytes 2359304 | tf_op jit(solution)/shard_map/ppermute | solution.py:13
  22.1 0.7 copy-start.2
  107.4 46.4 %collective-permute-start.3 = (f32[256,768]{1,0:T(8,128)S(1)}, f32[256,768]{1,0:T(8,128)S(1)}, u32[]{:S(2)}, u32[]{:S(2)}) collective-permute-start(f32[256,768]{1,0:T(8,128)S(1)} %add_multiply_fusion), channel_id=1, source_target_pairs={{0,512},{1,513},{2,514},{3,515},{4,516},{5,517},{6,518},{7,519},{8... | collective-permute-start | bytes 2359304 | tf_op jit(solution)/shard_map/ppermute | solution.py:13
  109.4 55.3 %collective-permute-start.2 = (f32[256,768]{1,0:T(8,128)S(1)}, f32[256,768]{1,0:T(8,128)S(1)}, u32[]{:S(2)}, u32[]{:S(2)}) collective-permute-start(f32[256,768]{1,0:T(8,128)S(1)} %convolution_multiply_fusion), channel_id=1, source_target_pairs={{0,516},{1,517},{2,518},{3,519},{4,512},{5,513},{6,514},{7,515},{8... | collective-permute-start | bytes 2359304 | tf_op jit(solution)/shard_map/ppermute | solution.py:13

commit v3 on v2

--- a/solution.py
+++ b/solution.py
@@ -4,7 +4,7 @@
 from jax.sharding import PartitionSpec as P
 
 EPS = 1e-06
-HIGH = lax.Precision.HIGHEST
+HIGH = lax.Precision.HIGH
 AXES = ("blk", "grp")
 
 
@@ -64,7 +64,9 @@
     far_back = exchanged(far_grad, far)
     near_back = exchanged(scale * (near_grad + times_transposed(slope[:, rows:], far_image)), near)
     text_grad = scale * (text_grad + times_transposed(slope[:, :rows], far_image))
-    return (norm_backward(image_emb, scale * image_grad + far_back), norm_backward(text_emb, text_grad + near_back))
+    image_out = norm_backward(image_emb, scale * image_grad + far_back)
+    image_out, text_grad = lax.optimization_barrier((image_out, text_grad))
+    return image_out, norm_backward(text_emb, text_grad + near_back)
 
 
 def solution(mesh):

time: 166 us -> 169 us (1.018)
  the two profiles are of different devices: /device:TPU:253 before, /device:TPU:127 now
where the time goes in v3:
time: 169 us
  waiting for transfers between devices  89.5 us (53%)
  starting transfers between devices  65 us (38%)
  matrix products  6.59 us (4%)
  other arithmetic  4.8 us (3%)
  between operations  2.12 us (1%)
    ppermute x4, waiting for transfers between devices, exchanged(): lax.ppermute(value, AXES, [(source, source ^ flip) for source in range(si...  89.5 us
    ppermute x4, starting transfers between devices, exchanged(): lax.ppermute(value, AXES, [(source, source ^ flip) for source in range(si...  65 us
  transfers between devices with their start and end apart: 4, of which 3 were waited for; matrix products, arithmetic and copies ran while one was open for 5% of the time, Pallas kernels for 0%

profile of v3, /device:TPU:127, one launch (start us, length us, event | category | flops | bytes accessed | tf_op | source)
XLA Modules:
  0.0 168.7 jit_solution(4056250216125543661)
XLA Ops:
  0.6 5.9 %collective-permute-start = (f32[256,768]{1,0:T(8,128)}, f32[256,768]{1,0:T(8,128)S(1)}, u32[]{:S(2)}, u32[]{:S(2)}) collective-permute-start(f32[256,768]{1,0:T(8,128)} %param.6), channel_id=1, source_target_pairs={{0,512},{1,513},{2,514},{3,515},{4,516},{5,517},{6,518},{7,519},{8... | collective-permute-start | bytes 2359304 | tf_op jit(solution)/shard_map/ppermute | solution.py:13
  6.6 14.6 %collective-permute-start.1 = (f32[256,768]{1,0:T(8,128)}, f32[256,768]{1,0:T(8,128)S(1)}, u32[]{:S(2)}, u32[]{:S(2)}) collective-permute-start(f32[256,768]{1,0:T(8,128)} %param.5), channel_id=1, source_target_pairs={{0,516},{1,517},{2,518},{3,519},{4,512},{5,513},{6,514},{7,515},{8... | collective-permute-start | bytes 2359304 | tf_op jit(solution)/shard_map/ppermute | solution.py:13
  21.2 1.3 multiply_reduce_fusion.4
  22.4 0.1 multiply_reduce_fusion.5
  24.0 0.5 copy-done.2
  24.6 0.6 fusion.13
  25.2 0.5 fusion.40
  25.7 0.6 fusion.25
  26.4 17.8 %collective-permute-done = f32[256,768]{1,0:T(8,128)S(1)} collective-permute-done((f32[256,768]{1,0:T(8,128)}, f32[256,768]{1,0:T(8,128)S(1)}, u32[]{:S(2)}, u32[]{:S(2)}) %collective-permute-start) | collective-permute-done | bytes 786464 | tf_op jit(solution)/shard_map/ppermute | solution.py:13
  44.5 0.6 fusion.17
  45.1 0.6 fusion.23
  45.7 0.5 convolution_add_fusion
  46.2 29.1 %collective-permute-done.1 = f32[256,768]{1,0:T(8,128)S(1)} collective-permute-done((f32[256,768]{1,0:T(8,128)}, f32[256,768]{1,0:T(8,128)S(1)}, u32[]{:S(2)}, u32[]{:S(2)}) %collective-permute-start.1) | collective-permute-done | bytes 786464 | tf_op jit(solution)/shard_map/ppermute | solution.py:13
  75.5 0.9 fusion.6
  76.5 0.9 convolution_multiply_fusion
  77.4 10.9 %collective-permute-start.2 = (f32[256,768]{1,0:T(8,128)S(1)}, f32[256,768]{1,0:T(8,128)S(1)}, u32[]{:S(2)}, u32[]{:S(2)}) collective-permute-start(f32[256,768]{1,0:T(8,128)S(1)} %convolution_multiply_fusion), channel_id=1, source_target_pairs={{0,516},{1,517},{2,518},{3,519},{4,512},{5,513},{6,514},{7,515},{8... | collective-permute-start | bytes 2359304 | tf_op jit(solution)/shard_map/ppermute | solution.py:13
  88.3 0.6 fusion.18
  89.0 33.6 %collective-permute-start.3 = (f32[256,768]{1,0:T(8,128)S(1)}, f32[256,768]{1,0:T(8,128)S(1)}, u32[]{:S(2)}, u32[]{:S(2)}) collective-permute-start(f32[256,768]{1,0:T(8,128)S(1)} %add_multiply_fusion), channel_id=1, source_target_pairs={{0,512},{1,513},{2,514},{3,515},{4,516},{5,517},{6,518},{7,519},{8... | collective-permute-start | bytes 2359304 | tf_op jit(solution)/shard_map/ppermute | solution.py:13
  122.6 0.6 fusion.20
  123.4 42.6 %collective-permute-done.2 = f32[256,768]{1,0:T(8,128)S(1)} collective-permute-done((f32[256,768]{1,0:T(8,128)S(1)}, f32[256,768]{1,0:T(8,128)S(1)}, u32[]{:S(2)}, u32[]{:S(2)}) %collective-permute-start.2) | collective-permute-done | bytes 786464 | tf_op jit(solution)/shard_map/ppermute | solution.py:13
  166.0 0.3 multiply_reduce_fusion.1
  166.2 1.1 subtract_multiply_fusion.1
  167.3 0.2 multiply_reduce_fusion
  167.6 1.1 subtract_multiply_fusion
  (16 shorter events, 0.8 us)
Async XLA Ops:
  0.6 21.8 %copy-start = (f32[256,768]{1,0:T(8,128)S(1)}, f32[256,768]{1,0:T(8,128)}, u32[]{:S(2)}) copy-start(f32[256,768]{1,0:T(8,128)} %param.5) | copy-start | bytes 2359300
  0.6 23.3 %copy-start.1 = (f32[256,768]{1,0:T(8,128)S(1)}, f32[256,768]{1,0:T(8,128)}, u32[]{:S(2)}) copy-start(f32[256,768]{1,0:T(8,128)} %param.6) | copy-start | bytes 2359300
  0.6 43.5 %collective-permute-start = (f32[256,768]{1,0:T(8,128)}, f32[256,768]{1,0:T(8,128)S(1)}, u32[]{:S(2)}, u32[]{:S(2)}) collective-permute-start(f32[256,768]{1,0:T(8,128)} %param.6), channel_id=1, source_target_pairs={{0,512},{1,513},{2,514},{3,515},{4,516},{5,517},{6,518},{7,519},{8... | collective-permute-start | bytes 2359304 | tf_op jit(solution)/shard_map/ppermute | solution.py:13
  6.6 68.8 %collective-permute-start.1 = (f32[256,768]{1,0:T(8,128)}, f32[256,768]{1,0:T(8,128)S(1)}, u32[]{:S(2)}, u32[]{:S(2)}) collective-permute-start(f32[256,768]{1,0:T(8,128)} %param.5), channel_id=1, source_target_pairs={{0,516},{1,517},{2,518},{3,519},{4,512},{5,513},{6,514},{7,515},{8... | collective-permute-start | bytes 2359304 | tf_op jit(solution)/shard_map/ppermute | solution.py:13
  23.9 0.7 copy-start.2
  77.4 88.6 %collective-permute-start.2 = (f32[256,768]{1,0:T(8,128)S(1)}, f32[256,768]{1,0:T(8,128)S(1)}, u32[]{:S(2)}, u32[]{:S(2)}) collective-permute-start(f32[256,768]{1,0:T(8,128)S(1)} %convolution_multiply_fusion), channel_id=1, source_target_pairs={{0,516},{1,517},{2,518},{3,519},{4,512},{5,513},{6,514},{7,515},{8... | collective-permute-start | bytes 2359304 | tf_op jit(solution)/shard_map/ppermute | solution.py:13
  89.0 78.3 %collective-permute-start.3 = (f32[256,768]{1,0:T(8,128)S(1)}, f32[256,768]{1,0:T(8,128)S(1)}, u32[]{:S(2)}, u32[]{:S(2)}) collective-permute-start(f32[256,768]{1,0:T(8,128)S(1)} %add_multiply_fusion), channel_id=1, source_target_pairs={{0,512},{1,513},{2,514},{3,515},{4,516},{5,517},{6,518},{7,519},{8... | collective-permute-start | bytes 2359304 | tf_op jit(solution)/shard_map/ppermute | solution.py:13

commit v4 on v3

--- a/solution.py
+++ b/solution.py
@@ -8,9 +8,18 @@
 AXES = ("blk", "grp")
 
 
-def exchanged(value, flip):
+def exchanged(far_value, near_value, far, near):
     size = lax.axis_size("blk") * lax.axis_size("grp")
-    return lax.ppermute(value, AXES, [(source, source ^ flip) for source in range(size)])
+    even = lax.axis_index("grp") % 2 == 0
+
+    def permuted(value, even_flip, odd_flip):
+        return lax.ppermute(value, AXES, [(source, source ^ (odd_flip if source % 2 else even_flip)) for source in range(size)])
+
+    values = jnp.where(even, far_value, near_value), jnp.where(even, near_value, far_value)
+    *values, far_value, near_value = lax.optimization_barrier((*values, far_value, near_value))
+    first = permuted(values[0], far, near)
+    second = permuted(values[1], near, far)
+    return far_value, near_value, jnp.where(even, first, second), jnp.where(even, second, first)
 
 
 def unit_rows(rows):
@@ -42,8 +51,7 @@
     def slopes(images, texts):
         return jax.nn.sigmoid(scale * jnp.einsum("rd,cd->rc", images, texts, precision=HIGH) + bias)
 
-    near_emb = exchanged(text_emb, near)
-    far_emb = exchanged(image_emb, far)
+    image_emb, text_emb, far_emb, near_emb = exchanged(image_emb, text_emb, far, near)
 
     image, text = unit_rows(image_emb), unit_rows(text_emb)
     columns = jnp.arange(rows, dtype=jnp.int32)
@@ -52,21 +60,18 @@
     text_grad = times_transposed(slope, image)
 
     near_text = unit_rows(near_emb)
+    far_image = unit_rows(far_emb)
     slope = slopes(image, near_text)
     image_grad = image_grad + times(slope, near_text)
     near_grad = times_transposed(slope, image)
-    image_grad, text_grad, near_grad, near_text = lax.optimization_barrier((image_grad, text_grad, near_grad, near_text))
 
-    far_image = unit_rows(far_emb)
     texts = jnp.concatenate([text, near_text], 0)
     slope = slopes(far_image, texts)
-    far_grad, slope = lax.optimization_barrier((scale * times(slope, texts), slope))
-    far_back = exchanged(far_grad, far)
-    near_back = exchanged(scale * (near_grad + times_transposed(slope[:, rows:], far_image)), near)
+    far_grad = scale * times(slope, texts)
+    near_grad = scale * (near_grad + times_transposed(slope[:, rows:], far_image))
+    _, _, far_back, near_back = exchanged(far_grad, near_grad, far, near)
     text_grad = scale * (text_grad + times_transposed(slope[:, :rows], far_image))
-    image_out = norm_backward(image_emb, scale * image_grad + far_back)
-    image_out, text_grad = lax.optimization_barrier((image_out, text_grad))
-    return image_out, norm_backward(text_emb, text_grad + near_back)
+    return norm_backward(image_emb, scale * image_grad + far_back), norm_backward(text_emb, text_grad + near_back)
 
 
 def solution(mesh):

time: 169 us -> 175 us (1.036)
  the two profiles are of different devices: /device:TPU:127 before, /device:TPU:1 now
where the time goes in v4:
time: 175 us
  waiting for transfers between devices  126 us (72%)
  starting transfers between devices  34.8 us (20%)
  matrix products  7.35 us (4%)
  other arithmetic  4.47 us (3%)
  between operations  2.13 us (1%)
    ppermute x4, waiting for transfers between devices, permuted(): lax.ppermute(value, AXES, [(source, source ^ (odd_flip if source % 2 else...  126 us
    ppermute x4, starting transfers between devices, permuted(): lax.ppermute(value, AXES, [(source, source ^ (odd_flip if source % 2 else...  34.8 us
  transfers between devices with their start and end apart: 4, of which 4 were waited for; matrix products, arithmetic and copies ran while one was open for 1% of the time, Pallas kernels for 0%

profile of v4, /device:TPU:1, one launch (start us, length us, event | category | flops | bytes accessed | tf_op | source)
XLA Modules:
  0.0 175.2 jit_solution(2493713856858059680)
XLA Ops:
  0.7 1.6 broadcast_select_fusion.4
  2.3 6.6 %collective-permute-start.1 = (f32[256,768]{1,0:T(8,128)S(1)}, f32[256,768]{1,0:T(8,128)S(1)}, u32[]{:S(2)}, u32[]{:S(2)}) collective-permute-start(f32[256,768]{1,0:T(8,128)S(1)} %get-tuple-element.11), channel_id=1, source_target_pairs={{0,516},{1,513},{2,518},{3,515},{4,512},{5,517},{6,514},{7,519},{8... | collective-permute-start | bytes 2359304 | tf_op jit(solution)/shard_map/ppermute | solution.py:16
  8.9 15.5 %collective-permute-start = (f32[256,768]{1,0:T(8,128)S(1)}, f32[256,768]{1,0:T(8,128)S(1)}, u32[]{:S(2)}, u32[]{:S(2)}) collective-permute-start(f32[256,768]{1,0:T(8,128)S(1)} %get-tuple-element.10), channel_id=1, source_target_pairs={{0,512},{1,517},{2,514},{3,519},{4,516},{5,513},{6,518},{7,515},{8... | collective-permute-start | bytes 2359304 | tf_op jit(solution)/shard_map/ppermute | solution.py:16
  24.4 0.2 multiply_reduce_fusion.4
  26.0 0.8 collective-permute-done.1
  26.8 64.1 %collective-permute-done = f32[256,768]{1,0:T(8,128)S(1)} collective-permute-done((f32[256,768]{1,0:T(8,128)S(1)}, f32[256,768]{1,0:T(8,128)S(1)}, u32[]{:S(2)}, u32[]{:S(2)}) %collective-permute-start) | collective-permute-done | bytes 786464 | tf_op jit(solution)/shard_map/ppermute | solution.py:16
  90.9 0.2 multiply_reduce_fusion.3
  91.0 0.3 multiply_reduce_fusion.2
  91.3 0.6 fusion.22
  91.9 0.6 fusion.28
  92.6 1.0 fusion.11
  93.6 0.9 convolution_multiply_fusion
  94.5 0.7 broadcast_select_fusion
  95.2 2.9 %collective-permute-start.2 = (f32[256,768]{1,0:T(8,128)S(1)}, f32[256,768]{1,0:T(8,128)S(1)}, u32[]{:S(2)}, u32[]{:S(2)}) collective-permute-start(f32[256,768]{1,0:T(8,128)S(1)} %get-tuple-element.12), channel_id=1, source_target_pairs={{0,516},{1,513},{2,518},{3,515},{4,512},{5,517},{6,514},{7,519},{8... | collective-permute-start | bytes 2359304 | tf_op jit(solution)/shard_map/ppermute | solution.py:16
  98.1 9.8 %collective-permute-start.3 = (f32[256,768]{1,0:T(8,128)S(1)}, f32[256,768]{1,0:T(8,128)S(1)}, u32[]{:S(2)}, u32[]{:S(2)}) collective-permute-start(f32[256,768]{1,0:T(8,128)S(1)} %get-tuple-element.13), channel_id=1, source_target_pairs={{0,512},{1,517},{2,514},{3,519},{4,516},{5,513},{6,518},{7,515},{8... | collective-permute-start | bytes 2359304 | tf_op jit(solution)/shard_map/ppermute | solution.py:16
  107.9 0.6 fusion.18
  108.5 0.6 fusion.43
  109.1 0.6 fusion.26
  109.7 49.9 %collective-permute-done.2 = f32[256,768]{1,0:T(8,128)S(1)} collective-permute-done((f32[256,768]{1,0:T(8,128)S(1)}, f32[256,768]{1,0:T(8,128)S(1)}, u32[]{:S(2)}, u32[]{:S(2)}) %collective-permute-start.2) | collective-permute-done | bytes 786464 | tf_op jit(solution)/shard_map/ppermute | solution.py:16
  159.6 11.7 %collective-permute-done.3 = f32[256,768]{1,0:T(8,128)S(1)} collective-permute-done((f32[256,768]{1,0:T(8,128)S(1)}, f32[256,768]{1,0:T(8,128)S(1)}, u32[]{:S(2)}, u32[]{:S(2)}) %collective-permute-start.3) | collective-permute-done | bytes 786464 | tf_op jit(solution)/shard_map/ppermute | solution.py:16
  171.4 0.9 multiply_reduce_fusion.1
  172.2 1.1 subtract_multiply_fusion.1
  173.3 0.8 multiply_reduce_fusion
  174.1 1.1 subtract_multiply_fusion
  (11 shorter events, 0.2 us)
Async XLA Ops:
  0.6 23.7 %copy-start = (f32[256,768]{1,0:T(8,128)S(1)}, f32[256,768]{1,0:T(8,128)}, u32[]{:S(2)}) copy-start(f32[256,768]{1,0:T(8,128)} %param.5) | copy-start | bytes 2359300
  0.7 23.7 %copy-start.1 = (f32[256,768]{1,0:T(8,128)S(1)}, f32[256,768]{1,0:T(8,128)}, u32[]{:S(2)}) copy-start(f32[256,768]{1,0:T(8,128)} %param.6) | copy-start | bytes 2359300
  2.3 24.5 %collective-permute-start.1 = (f32[256,768]{1,0:T(8,128)S(1)}, f32[256,768]{1,0:T(8,128)S(1)}, u32[]{:S(2)}, u32[]{:S(2)}) collective-permute-start(f32[256,768]{1,0:T(8,128)S(1)} %get-tuple-element.11), channel_id=1, source_target_pairs={{0,516},{1,513},{2,518},{3,515},{4,512},{5,517},{6,514},{7,519},{8... | collective-permute-start | bytes 2359304 | tf_op jit(solution)/shard_map/ppermute | solution.py:16
  8.9 82.0 %collective-permute-start = (f32[256,768]{1,0:T(8,128)S(1)}, f32[256,768]{1,0:T(8,128)S(1)}, u32[]{:S(2)}, u32[]{:S(2)}) collective-permute-start(f32[256,768]{1,0:T(8,128)S(1)} %get-tuple-element.10), channel_id=1, source_target_pairs={{0,512},{1,517},{2,514},{3,519},{4,516},{5,513},{6,518},{7,515},{8... | collective-permute-start | bytes 2359304 | tf_op jit(solution)/shard_map/ppermute | solution.py:16
  94.5 13.4 %copy-start.2 = (s32[256]{0:T(256)S(1)}, s32[256]{0:T(256)}, u32[]{:S(2)}) copy-start(s32[256]{0:T(256)} %param.7) | copy-start | bytes 3076
  95.2 64.4 %collective-permute-start.2 = (f32[256,768]{1,0:T(8,128)S(1)}, f32[256,768]{1,0:T(8,128)S(1)}, u32[]{:S(2)}, u32[]{:S(2)}) collective-permute-start(f32[256,768]{1,0:T(8,128)S(1)} %get-tuple-element.12), channel_id=1, source_target_pairs={{0,516},{1,513},{2,518},{3,515},{4,512},{5,517},{6,514},{7,519},{8... | collective-permute-start | bytes 2359304 | tf_op jit(solution)/shard_map/ppermute | solution.py:16
  98.1 73.3 %collective-permute-start.3 = (f32[256,768]{1,0:T(8,128)S(1)}, f32[256,768]{1,0:T(8,128)S(1)}, u32[]{:S(2)}, u32[]{:S(2)}) collective-permute-start(f32[256,768]{1,0:T(8,128)S(1)} %get-tuple-element.13), channel_id=1, source_target_pairs={{0,512},{1,517},{2,514},{3,519},{4,516},{5,513},{6,518},{7,515},{8... | collective-permute-start | bytes 2359304 | tf_op jit(solution)/shard_map/ppermute | solution.py:16

commit v5 on v4

--- a/solution.py
+++ b/solution.py
@@ -8,18 +8,9 @@
 AXES = ("blk", "grp")
 
 
-def exchanged(far_value, near_value, far, near):
+def permuted(value, even_flip, odd_flip):
     size = lax.axis_size("blk") * lax.axis_size("grp")
-    even = lax.axis_index("grp") % 2 == 0
-
-    def permuted(value, even_flip, odd_flip):
-        return lax.ppermute(value, AXES, [(source, source ^ (odd_flip if source % 2 else even_flip)) for source in range(size)])
-
-    values = jnp.where(even, far_value, near_value), jnp.where(even, near_value, far_value)
-    *values, far_value, near_value = lax.optimization_barrier((*values, far_value, near_value))
-    first = permuted(values[0], far, near)
-    second = permuted(values[1], near, far)
-    return far_value, near_value, jnp.where(even, first, second), jnp.where(even, second, first)
+    return lax.ppermute(value, AXES, [(source, source ^ (odd_flip if source % 2 else even_flip)) for source in range(size)])
 
 
 def unit_rows(rows):
@@ -51,7 +42,12 @@
     def slopes(images, texts):
         return jax.nn.sigmoid(scale * jnp.einsum("rd,cd->rc", images, texts, precision=HIGH) + bias)
 
-    image_emb, text_emb, far_emb, near_emb = exchanged(image_emb, text_emb, far, near)
+    odd = lax.axis_index("grp") % 2 == 1
+    sent = jnp.where(odd, image_emb, text_emb), jnp.where(odd, text_emb, image_emb)
+    *sent, image_emb, text_emb = lax.optimization_barrier((*sent, image_emb, text_emb))
+    first = permuted(sent[0], near, far)
+    second = permuted(sent[1], far, near)
+    near_emb, far_emb = jnp.where(odd, second, first), jnp.where(odd, first, second)
 
     image, text = unit_rows(image_emb), unit_rows(text_emb)
     columns = jnp.arange(rows, dtype=jnp.int32)
@@ -69,9 +65,12 @@
     slope = slopes(far_image, texts)
     far_grad = scale * times(slope, texts)
     near_grad = scale * (near_grad + times_transposed(slope[:, rows:], far_image))
-    _, _, far_back, near_back = exchanged(far_grad, near_grad, far, near)
+    far_back = permuted(far_grad, far, far)
+    near_back = permuted(near_grad, near, near)
     text_grad = scale * (text_grad + times_transposed(slope[:, :rows], far_image))
-    return norm_backward(image_emb, scale * image_grad + far_back), norm_backward(text_emb, text_grad + near_back)
+    text_out = norm_backward(text_emb, text_grad + near_back)
+    text_out, image_grad = lax.optimization_barrier((text_out, scale * image_grad))
+    return norm_backward(image_emb, image_grad + far_back), text_out
 
 
 def solution(mesh):

time: 175 us -> 176 us (level); the launches traced: 175 us -> 174 us
  waiting for transfers between devices: 126 us -> 104 us
  starting transfers between devices: 34.8 us -> 56.2 us
    ppermute x4, waiting for transfers between devices: 126 us -> 104 us  [permuted(): lax.ppermute(value, AXES, [(source, source ^ (odd_flip if source % 2 else...]
    ppermute x4, starting transfers between devices: 34.8 us -> 56.2 us  [permuted(): lax.ppermute(value, AXES, [(source, source ^ (odd_flip if source % 2 else...]
  transfers between devices with their start and end apart: 4 -> 4, of which waited for: 4 -> 3; matrix products, arithmetic and copies ran while one was open for 1% -> 3% of each run, Pallas kernels for 0% -> 0%
where the time goes in v5:
time: 176 us; the launch traced here: 174 us
  waiting for transfers between devices  104 us (59%)
  starting transfers between devices  56.2 us (32%)
  matrix products  6.92 us (4%)
  other arithmetic  4.75 us (3%)
  between operations  2.13 us (1%)
    ppermute x4, waiting for transfers between devices, permuted(): lax.ppermute(value, AXES, [(source, source ^ (odd_flip if source % 2 else...  104 us
    ppermute x4, starting transfers between devices, permuted(): lax.ppermute(value, AXES, [(source, source ^ (odd_flip if source % 2 else...  56.2 us
  transfers between devices with their start and end apart: 4, of which 3 were waited for; matrix products, arithmetic and copies ran while one was open for 3% of the time, Pallas kernels for 0%

profile of v5, /device:TPU:1, one launch (start us, length us, event | category | flops | bytes accessed | tf_op | source)
XLA Modules:
  0.0 174.4 jit_solution(7427925691147992868)
XLA Ops:
  0.7 1.5 broadcast_select_fusion.2
  2.2 20.1 %collective-permute-start = (f32[256,768]{1,0:T(8,128)S(1)}, f32[256,768]{1,0:T(8,128)S(1)}, u32[]{:S(2)}, u32[]{:S(2)}) collective-permute-start(f32[256,768]{1,0:T(8,128)S(1)} %get-tuple-element.10), channel_id=1, source_target_pairs={{0,512},{1,517},{2,514},{3,519},{4,516},{5,513},{6,518},{7,515},{8... | collective-permute-start | bytes 2359304 | tf_op jit(solution)/shard_map/ppermute | solution.py:13
  22.3 2.2 %collective-permute-start.1 = (f32[256,768]{1,0:T(8,128)S(1)}, f32[256,768]{1,0:T(8,128)S(1)}, u32[]{:S(2)}, u32[]{:S(2)}) collective-permute-start(f32[256,768]{1,0:T(8,128)S(1)} %get-tuple-element.11), channel_id=1, source_target_pairs={{0,516},{1,513},{2,518},{3,515},{4,512},{5,517},{6,514},{7,519},{8... | collective-permute-start | bytes 2359304 | tf_op jit(solution)/shard_map/ppermute | solution.py:13
  26.2 0.5 copy-done.2
  26.8 0.6 fusion.17
  27.4 0.6 fusion.28
  28.0 27.1 %collective-permute-done = f32[256,768]{1,0:T(8,128)S(1)} collective-permute-done((f32[256,768]{1,0:T(8,128)S(1)}, f32[256,768]{1,0:T(8,128)S(1)}, u32[]{:S(2)}, u32[]{:S(2)}) %collective-permute-start) | collective-permute-done | bytes 786464 | tf_op jit(solution)/shard_map/ppermute | solution.py:13
  55.2 9.1 %collective-permute-done.1 = f32[256,768]{1,0:T(8,128)S(1)} collective-permute-done((f32[256,768]{1,0:T(8,128)S(1)}, f32[256,768]{1,0:T(8,128)S(1)}, u32[]{:S(2)}, u32[]{:S(2)}) %collective-permute-start.1) | collective-permute-done | bytes 786464 | tf_op jit(solution)/shard_map/ppermute | solution.py:13
  64.3 0.2 multiply_reduce_fusion.2
  64.4 0.3 multiply_reduce_fusion.3
  64.7 0.6 fusion.21
  65.3 0.6 fusion.25
  66.0 1.0 fusion.10
  67.0 0.6 fusion.1
  67.6 4.4 %collective-permute-start.2 = (f32[256,768]{1,0:T(8,128)S(1)}, f32[256,768]{1,0:T(8,128)S(1)}, u32[]{:S(2)}, u32[]{:S(2)}) collective-permute-start(f32[256,768]{1,0:T(8,128)S(1)} %fusion.1), channel_id=1, source_target_pairs={{0,512},{1,513},{2,514},{3,515},{4,516},{5,517},{6,518},{7,519},{8... | collective-permute-start | bytes 2359304 | tf_op jit(solution)/shard_map/ppermute | solution.py:13
  72.0 0.6 fusion.42
  72.6 0.9 convolution_multiply_fusion
  73.5 29.6 %collective-permute-start.3 = (f32[256,768]{1,0:T(8,128)S(1)}, f32[256,768]{1,0:T(8,128)S(1)}, u32[]{:S(2)}, u32[]{:S(2)}) collective-permute-start(f32[256,768]{1,0:T(8,128)S(1)} %convolution_multiply_fusion), channel_id=1, source_target_pairs={{0,516},{1,517},{2,518},{3,519},{4,512},{5,513},{6,514},{7,515},{8... | collective-permute-start | bytes 2359304 | tf_op jit(solution)/shard_map/ppermute | solution.py:13
  103.1 0.6 fusion
  103.7 0.8 multiply_reduce_fusion.1
  104.4 1.1 subtract_multiply_fusion.1
  105.5 67.6 %collective-permute-done.3 = f32[256,768]{1,0:T(8,128)S(1)} collective-permute-done((f32[256,768]{1,0:T(8,128)S(1)}, f32[256,768]{1,0:T(8,128)S(1)}, u32[]{:S(2)}, u32[]{:S(2)}) %collective-permute-start.3) | collective-permute-done | bytes 786464 | tf_op jit(solution)/shard_map/ppermute | solution.py:13
  173.1 0.2 multiply_reduce_fusion
  173.4 1.1 subtract_multiply_fusion
  (13 shorter events, 0.4 us)
Async XLA Ops:
  0.6 23.8 %copy-start = (f32[256,768]{1,0:T(8,128)S(1)}, f32[256,768]{1,0:T(8,128)}, u32[]{:S(2)}) copy-start(f32[256,768]{1,0:T(8,128)} %param.5) | copy-start | bytes 2359300
  2.2 22.4 %copy-start.1 = (f32[256,768]{1,0:T(8,128)S(1)}, f32[256,768]{1,0:T(8,128)}, u32[]{:S(2)}) copy-start(f32[256,768]{1,0:T(8,128)} %param.6) | copy-start | bytes 2359300
  2.2 53.0 %collective-permute-start = (f32[256,768]{1,0:T(8,128)S(1)}, f32[256,768]{1,0:T(8,128)S(1)}, u32[]{:S(2)}, u32[]{:S(2)}) collective-permute-start(f32[256,768]{1,0:T(8,128)S(1)} %get-tuple-element.10), channel_id=1, source_target_pairs={{0,512},{1,517},{2,514},{3,519},{4,516},{5,513},{6,518},{7,515},{8... | collective-permute-start | bytes 2359304 | tf_op jit(solution)/shard_map/ppermute | solution.py:13
  22.3 42.0 %collective-permute-start.1 = (f32[256,768]{1,0:T(8,128)S(1)}, f32[256,768]{1,0:T(8,128)S(1)}, u32[]{:S(2)}, u32[]{:S(2)}) collective-permute-start(f32[256,768]{1,0:T(8,128)S(1)} %get-tuple-element.11), channel_id=1, source_target_pairs={{0,516},{1,513},{2,518},{3,515},{4,512},{5,517},{6,514},{7,519},{8... | collective-permute-start | bytes 2359304 | tf_op jit(solution)/shard_map/ppermute | solution.py:13
  26.1 0.7 copy-start.2
  67.6 36.1 %collective-permute-start.2 = (f32[256,768]{1,0:T(8,128)S(1)}, f32[256,768]{1,0:T(8,128)S(1)}, u32[]{:S(2)}, u32[]{:S(2)}) collective-permute-start(f32[256,768]{1,0:T(8,128)S(1)} %fusion.1), channel_id=1, source_target_pairs={{0,512},{1,513},{2,514},{3,515},{4,516},{5,517},{6,518},{7,519},{8... | collective-permute-start | bytes 2359304 | tf_op jit(solution)/shard_map/ppermute | solution.py:13
  73.5 99.6 %collective-permute-start.3 = (f32[256,768]{1,0:T(8,128)S(1)}, f32[256,768]{1,0:T(8,128)S(1)}, u32[]{:S(2)}, u32[]{:S(2)}) collective-permute-start(f32[256,768]{1,0:T(8,128)S(1)} %convolution_multiply_fusion), channel_id=1, source_target_pairs={{0,516},{1,517},{2,518},{3,519},{4,512},{5,513},{6,514},{7,515},{8... | collective-permute-start | bytes 2359304 | tf_op jit(solution)/shard_map/ppermute | solution.py:13

commit v6 on v2

--- a/solution.py
+++ b/solution.py
@@ -4,7 +4,7 @@
 from jax.sharding import PartitionSpec as P
 
 EPS = 1e-06
-HIGH = lax.Precision.HIGHEST
+HIGH = lax.Precision.HIGH
 AXES = ("blk", "grp")
 
 

time: 166 us -> 166 us (level)
  the two profiles are of different devices: /device:TPU:253 before, /device:TPU:237 now
where the time goes in v6:
time: 166 us
  waiting for transfers between devices  120 us (72%)
  starting transfers between devices  31.9 us (19%)
  matrix products  6.58 us (4%)
  other arithmetic  4.72 us (3%)
  between operations  2.12 us (1%)
    ppermute x4, waiting for transfers between devices, exchanged(): lax.ppermute(value, AXES, [(source, source ^ flip) for source in range(si...  120 us
    ppermute x4, starting transfers between devices, exchanged(): lax.ppermute(value, AXES, [(source, source ^ flip) for source in range(si...  31.9 us
  transfers between devices with their start and end apart: 4, of which 4 were waited for; matrix products, arithmetic and copies ran while one was open for 4% of the time, Pallas kernels for 0%

profile of v6, /device:TPU:237, one launch (start us, length us, event | category | flops | bytes accessed | tf_op | source)
XLA Modules:
  0.0 166.0 jit_solution(6972920262835689806)
XLA Ops:
  0.6 2.1 %collective-permute-start = (f32[256,768]{1,0:T(8,128)}, f32[256,768]{1,0:T(8,128)S(1)}, u32[]{:S(2)}, u32[]{:S(2)}) collective-permute-start(f32[256,768]{1,0:T(8,128)} %param.6), channel_id=1, source_target_pairs={{0,512},{1,513},{2,514},{3,515},{4,516},{5,517},{6,518},{7,519},{8... | collective-permute-start | bytes 2359304 | tf_op jit(solution)/shard_map/ppermute | solution.py:13
  2.7 16.7 %collective-permute-start.1 = (f32[256,768]{1,0:T(8,128)}, f32[256,768]{1,0:T(8,128)S(1)}, u32[]{:S(2)}, u32[]{:S(2)}) collective-permute-start(f32[256,768]{1,0:T(8,128)} %param.5), channel_id=1, source_target_pairs={{0,516},{1,517},{2,518},{3,519},{4,512},{5,513},{6,514},{7,515},{8... | collective-permute-start | bytes 2359304 | tf_op jit(solution)/shard_map/ppermute | solution.py:13
  19.4 1.3 multiply_reduce_fusion.4
  22.2 0.5 copy-done.2
  22.8 0.6 fusion.13
  23.4 0.5 fusion.40
  23.9 0.6 fusion.25
  24.6 18.9 %collective-permute-done = f32[256,768]{1,0:T(8,128)S(1)} collective-permute-done((f32[256,768]{1,0:T(8,128)}, f32[256,768]{1,0:T(8,128)S(1)}, u32[]{:S(2)}, u32[]{:S(2)}) %collective-permute-start) | collective-permute-done | bytes 786464 | tf_op jit(solution)/shard_map/ppermute | solution.py:13
  43.7 0.6 fusion.17
  44.3 0.6 fusion.23
  45.0 0.6 convolution_add_fusion
  45.5 57.5 %collective-permute-done.1 = f32[256,768]{1,0:T(8,128)S(1)} collective-permute-done((f32[256,768]{1,0:T(8,128)}, f32[256,768]{1,0:T(8,128)S(1)}, u32[]{:S(2)}, u32[]{:S(2)}) %collective-permute-start.1) | collective-permute-done | bytes 786464 | tf_op jit(solution)/shard_map/ppermute | solution.py:13
  103.2 0.9 fusion.6
  104.1 0.9 convolution_multiply_fusion
  105.0 0.6 fusion.18
  105.7 1.9 %collective-permute-start.3 = (f32[256,768]{1,0:T(8,128)S(1)}, f32[256,768]{1,0:T(8,128)S(1)}, u32[]{:S(2)}, u32[]{:S(2)}) collective-permute-start(f32[256,768]{1,0:T(8,128)S(1)} %add_multiply_fusion), channel_id=1, source_target_pairs={{0,512},{1,513},{2,514},{3,515},{4,516},{5,517},{6,518},{7,519},{8... | collective-permute-start | bytes 2359304 | tf_op jit(solution)/shard_map/ppermute | solution.py:13
  107.7 11.3 %collective-permute-start.2 = (f32[256,768]{1,0:T(8,128)S(1)}, f32[256,768]{1,0:T(8,128)S(1)}, u32[]{:S(2)}, u32[]{:S(2)}) collective-permute-start(f32[256,768]{1,0:T(8,128)S(1)} %convolution_multiply_fusion), channel_id=1, source_target_pairs={{0,516},{1,517},{2,518},{3,519},{4,512},{5,513},{6,514},{7,515},{8... | collective-permute-start | bytes 2359304 | tf_op jit(solution)/shard_map/ppermute | solution.py:13
  119.0 0.6 fusion.20
  119.6 34.4 %collective-permute-done.3 = f32[256,768]{1,0:T(8,128)S(1)} collective-permute-done((f32[256,768]{1,0:T(8,128)S(1)}, f32[256,768]{1,0:T(8,128)S(1)}, u32[]{:S(2)}, u32[]{:S(2)}) %collective-permute-start.3) | collective-permute-done | bytes 786464 | tf_op jit(solution)/shard_map/ppermute | solution.py:13
  153.9 0.3 multiply_reduce_fusion
  154.2 1.1 subtract_multiply_fusion
  155.3 9.3 %collective-permute-done.2 = f32[256,768]{1,0:T(8,128)S(1)} collective-permute-done((f32[256,768]{1,0:T(8,128)S(1)}, f32[256,768]{1,0:T(8,128)S(1)}, u32[]{:S(2)}, u32[]{:S(2)}) %collective-permute-start.2) | collective-permute-done | bytes 786464 | tf_op jit(solution)/shard_map/ppermute | solution.py:13
  164.6 0.3 multiply_reduce_fusion.1
  164.9 1.1 subtract_multiply_fusion.1
  (15 shorter events, 0.8 us)
Async XLA Ops:
  0.6 20.0 %copy-start = (f32[256,768]{1,0:T(8,128)S(1)}, f32[256,768]{1,0:T(8,128)}, u32[]{:S(2)}) copy-start(f32[256,768]{1,0:T(8,128)} %param.5) | copy-start | bytes 2359300
  0.6 21.5 %copy-start.1 = (f32[256,768]{1,0:T(8,128)S(1)}, f32[256,768]{1,0:T(8,128)}, u32[]{:S(2)}) copy-start(f32[256,768]{1,0:T(8,128)} %param.6) | copy-start | bytes 2359300
  0.6 42.8 %collective-permute-start = (f32[256,768]{1,0:T(8,128)}, f32[256,768]{1,0:T(8,128)S(1)}, u32[]{:S(2)}, u32[]{:S(2)}) collective-permute-start(f32[256,768]{1,0:T(8,128)} %param.6), channel_id=1, source_target_pairs={{0,512},{1,513},{2,514},{3,515},{4,516},{5,517},{6,518},{7,519},{8... | collective-permute-start | bytes 2359304 | tf_op jit(solution)/shard_map/ppermute | solution.py:13
  2.7 100.3 %collective-permute-start.1 = (f32[256,768]{1,0:T(8,128)}, f32[256,768]{1,0:T(8,128)S(1)}, u32[]{:S(2)}, u32[]{:S(2)}) collective-permute-start(f32[256,768]{1,0:T(8,128)} %param.5), channel_id=1, source_target_pairs={{0,516},{1,517},{2,518},{3,519},{4,512},{5,513},{6,514},{7,515},{8... | collective-permute-start | bytes 2359304 | tf_op jit(solution)/shard_map/ppermute | solution.py:13
  22.1 0.7 copy-start.2
  105.7 48.2 %collective-permute-start.3 = (f32[256,768]{1,0:T(8,128)S(1)}, f32[256,768]{1,0:T(8,128)S(1)}, u32[]{:S(2)}, u32[]{:S(2)}) collective-permute-start(f32[256,768]{1,0:T(8,128)S(1)} %add_multiply_fusion), channel_id=1, source_target_pairs={{0,512},{1,513},{2,514},{3,515},{4,516},{5,517},{6,518},{7,519},{8... | collective-permute-start | bytes 2359304 | tf_op jit(solution)/shard_map/ppermute | solution.py:13
  107.7 57.0 %collective-permute-start.2 = (f32[256,768]{1,0:T(8,128)S(1)}, f32[256,768]{1,0:T(8,128)S(1)}, u32[]{:S(2)}, u32[]{:S(2)}) collective-permute-start(f32[256,768]{1,0:T(8,128)S(1)} %convolution_multiply_fusion), channel_id=1, source_target_pairs={{0,516},{1,517},{2,518},{3,519},{4,512},{5,513},{6,514},{7,515},{8... | collective-permute-start | bytes 2359304 | tf_op jit(solution)/shard_map/ppermute | solution.py:13
